TPU v7x, 32 devices: a whole 2x2x4 slice. The times are simulated.
32 devices in a mesh: dom: 8 (over z, x), sub: 4 (over y, core).
Axes of the slice: x: 2, y: 2, z: 4, core: 2. Of those that a mesh axis runs over, the one named last changes fastest.
Arguments:
- initial_state: float32 [320, 8192], P(None, ('dom', 'sub')), may hold values from -6 to 6
- cotangent: float32 [320, 8192], P(None, ('dom', 'sub')), may hold values from -6 to 6
- volume_operator: bfloat16 [320, 320], replicated, may hold values from -0.3125 to 0.3125
- in_weight: bfloat16 [64, 10], replicated, may hold values from -2 to 2
- in_bias: float32 [64], replicated, may hold values from -3 to 3
- mid_weight: bfloat16 [64, 64], replicated, may hold values from -0.75 to 0.75
- mid_bias: float32 [64], replicated, may hold values from -3 to 3
- out_weight: bfloat16 [5, 64], replicated, may hold values from -0.75 to 0.75
- flux_matrix: float32 [5, 5], replicated, may hold values from -2.5 to 2.5
- dom_send: int32 [8, 1024], P('dom', 'sub'), may hold values from 0 to 1535
- dom_count: int32 [8, 32], P('dom', 'sub'), may hold values from 0 to 32, as said below
- sub_send: int32 [8, 2048], P('dom', 'sub'), may hold values from 0 to 1535
- partner: int32 [8, 6144], P('dom', 'sub'), may hold values from 0 to 2303, as said below
Outputs:
- final_state: float32 [320, 8192], P(None, ('dom', 'sub'))
- adjoint_state: float32 [320, 8192], P(None, ('dom', 'sub'))
Inputs may be any that keep to these rules, and one draw needn't show every extreme that they name: `dom_send`: local face slots, face*256+element. `dom_count`: counts of live slots; in every partition some block is full. `sub_send`: local face slots, face*256+element. `partner`: entries below 1536 name a local face slot; each received slot 6*256+r is named by exactly one face of the partition.
All inputs are finite; a program needn't handle non-finite values.
Results may differ from a plain program's by a relative error of at most 0.0033.
Values may be sent and summed in bfloat16 or wider, within the bound.
A program may use at most 64 MiB of HBM per device.

v0:
```python
import functools

import jax
import jax.numpy as jnp
import numpy as np
from jax import lax
from jax.experimental import pallas as pl
from jax.experimental.pallas import tpu as pltpu
from jax.sharding import PartitionSpec as P

REACH = 4
OFFSETS = [offset for offset in range(-REACH, REACH + 1) if offset != 0]
PAIRS = len(OFFSETS)
MESH = pl.DeviceIdType.MESH

time_step = 0.4
lift_gain = 1.5
BF = jnp.bfloat16
F32 = jnp.float32


def face_rows():
    table = np.zeros((6, 5, 16, 5, 64), np.float32)
    for k in range(16):
        low, high = k % 4, k // 4
        nodes = [
            4 * k,
            3 + 4 * k,
            low + 16 * high,
            low + 12 + 16 * high,
            k,
            k + 48,
        ]
        for f, node in enumerate(nodes):
            for v in range(5):
                table[f, v, k, v, node] = 1.0
    return table.reshape(480, 320)


def mm(a, b):
    return jnp.dot(a, b, preferred_element_type=F32)


def mm_nt(a, b):
    return lax.dot_general(a, b, (((1,), (1,)), ((), ())), preferred_element_type=F32)


def mm_tn(a, b):
    return lax.dot_general(a, b, (((0,), (0,)), ((), ())), preferred_element_type=F32)


def split(values):
    high = values.astype(BF)
    return high, (values - high.astype(F32)).astype(BF)


def to_wide(faces, elements):
    return jnp.concatenate([faces[f * 80 : (f + 1) * 80] for f in range(6)], axis=1)


def to_tall(wide, elements):
    return jnp.concatenate(
        [wide[:, f * elements : (f + 1) * elements] for f in range(6)], axis=0
    )


def lift(face_t, wide, elements):
    high, low = split(to_tall(wide, elements))
    return mm(face_t, high) + mm(face_t, low)


def mix(flux_ref, values, transposed):
    rows = []
    for v in range(5):
        total = None
        for u in range(5):
            weight = flux_ref[u, v] if transposed else flux_ref[v, u]
            term = weight * values[u * 16 : (u + 1) * 16]
            total = term if total is None else total + term
        rows.append(total)
    return jnp.concatenate(rows, axis=0)


def one_hot_rows(row_list, base, rows):
    width = row_list.shape[1]
    shifted = (row_list - base).astype(F32)
    wide = jnp.broadcast_to(shifted, (rows, width))
    spot = lax.broadcasted_iota(jnp.int32, (rows, width), 0).astype(F32)
    return jnp.where(wide == spot, 1.0, 0.0).astype(BF)


def kernel(
    n_dom,
    n_sub,
    w_ref,
    ct_ref,
    vol_op_ref,
    in_w_ref,
    in_b_ref,
    mid_w_ref,
    mid_b_ref,
    out_w_ref,
    flux_ref,
    dom_ref,
    count_ref,
    sub_ref,
    partner_ref,
    face_ref,
    face_t_ref,
    final_ref,
    adj_ref,
    pick,
    send_hot,
    w1,
    w1t,
    m4,
    m4t,
    o16,
    o16t,
    bias1,
    bias2,
    x_in,
    g_in,
    clo,
    x_grad,
    slope1,
    slope2,
    traces_s,
    near,
    grad_near,
    middle_s,
    adj_mid_s,
    out_buf,
    in_buf,
    dom_send_sem,
    dom_recv_sem,
    sub_send_sem,
    sub_recv_sem,
):
    elements = w_ref.shape[1]
    faces = 6 * elements
    dom_width = dom_ref.shape[1]
    peer_slots = dom_width // PAIRS
    sub_width = sub_ref.shape[1]
    sub_slots = sub_width // n_sub
    slots = dom_width + sub_width
    d = lax.axis_index("dom")
    s = lax.axis_index("sub")

    def inside(j):
        target = d + OFFSETS[j]
        return (target >= 0) & (target < n_dom)

    barrier = pltpu.get_barrier_semaphore()
    expected = n_sub - 1
    for j in range(PAIRS):
        expected = expected + jnp.where(inside(j), 1, 0)

        @pl.when(inside(j))
        def _():
            pl.semaphore_signal(
                barrier, inc=1, device_id=(d + OFFSETS[j], s), device_id_type=MESH
            )

    for step in range(1, n_sub):
        pl.semaphore_signal(
            barrier, inc=1, device_id=(d, lax.rem(s + step, n_sub)), device_id_type=MESH
        )

    def dom_copy(phase, j):
        rows = pl.ds(j * peer_slots, peer_slots)
        return pltpu.make_async_remote_copy(
            src_ref=out_buf.at[phase, rows],
            dst_ref=in_buf.at[phase, rows],
            send_sem=dom_send_sem.at[phase, j],
            recv_sem=dom_recv_sem.at[phase, j],
            device_id=(d + OFFSETS[j], s),
            device_id_type=MESH,
        )

    def sub_copy(phase, step):
        there = lax.rem(s + step, n_sub)
        source = pl.ds(pl.multiple_of(dom_width + there * sub_slots, 32), sub_slots)
        target = pl.ds(pl.multiple_of(dom_width + s * sub_slots, 32), sub_slots)
        return pltpu.make_async_remote_copy(
            src_ref=out_buf.at[phase, source],
            dst_ref=in_buf.at[phase, target],
            send_sem=sub_send_sem.at[phase, step - 1],
            recv_sem=sub_recv_sem.at[phase, step - 1],
            device_id=(d, there),
            device_id_type=MESH,
        )

    def start_exchange(phase):
        for j in range(PAIRS):

            @pl.when(inside(j))
            def _():
                dom_copy(phase, j).start()

        for step in range(1, n_sub):
            sub_copy(phase, step).start()
        own = pl.ds(pl.multiple_of(dom_width + s * sub_slots, 32), sub_slots)
        in_buf[phase, own, :] = out_buf[phase, own, :]

    def wait_exchange(phase):
        for j in range(PAIRS):
            @pl.when(inside(PAIRS - 1 - j))
            def _():
                dom_copy(phase, j).wait_recv()

            @pl.when(inside(j))
            def _():
                dom_copy(phase, j).wait_send()

            @pl.when(jnp.logical_not(inside(PAIRS - 1 - j)))
            def _():
                in_buf[phase, pl.ds(j * peer_slots, peer_slots), :] = jnp.zeros(
                    (peer_slots, 256), BF
                )

        for step in range(1, n_sub):
            sub_copy(phase, step).wait()

    def flip(rows):
        parts = [
            rows[j * peer_slots : (j + 1) * peer_slots] for j in reversed(range(PAIRS))
        ]
        return jnp.concatenate(parts + [rows[dom_width:]], axis=0)

    def slots_to_rows(values):
        padded = jnp.concatenate([values, jnp.zeros((48, slots), F32)], axis=0)
        return jnp.transpose(padded)

    def put_forward(phase, values):
        out_buf[phase, :, 0:128] = slots_to_rows(values).astype(BF)

    def put_backward(phase, values):
        out_buf[phase, :, 128:256] = flip(slots_to_rows(values)).astype(BF)

    def got_forward(phase):
        return jnp.transpose(in_buf[phase, :, 0:128].astype(F32))[:80].astype(BF)

    def got_backward(phase):
        rows = flip(in_buf[phase, :, 128:256].astype(F32))
        return jnp.transpose(rows)[:80].astype(BF)

    lane = lax.broadcasted_iota(jnp.int32, (1, dom_width), 1)
    dom_list = dom_ref[...]
    for j in range(PAIRS):
        dead = (lane >= j * peer_slots + count_ref[0, j]) & (lane < (j + 1) * peer_slots)
        dom_list = jnp.where(dead, -1, dom_list)
    send_list = jnp.concatenate([dom_list, sub_ref[...]], axis=1)
    for base in range(0, faces, 256):
        send_hot[pl.ds(base, 256), :] = one_hot_rows(send_list, base, 256)
    partner = partner_ref[...]
    for base in range(faces, faces + slots, 256):
        pick[pl.ds(base, 256), :] = one_hot_rows(partner, base, 256)

    face = face_ref[...]
    face_t = face_t_ref[...]

    def traces_of(field_b):
        return to_wide(mm(face, field_b), elements).astype(BF)

    def jump_grad_of(g):
        high, low = split(g)
        values = to_wide(mm(face, high) + mm(face, low), elements)
        return mix(flux_ref, lift_gain * values, True)

    pick_near = pick.at[pl.ds(0, faces)]
    pick_far = pick.at[pl.ds(faces, slots)]

    field0 = w_ref[...].astype(BF)
    traces0 = traces_of(field0)
    put_forward(0, mm(traces0, send_hot[...]))
    jump0 = jump_grad_of(ct_ref[...])
    jump0_b = jump0.astype(BF)
    put_backward(0, mm_nt(jump0_b, pick_far[...]))
    pl.semaphore_wait(barrier, expected)
    start_exchange(0)

    for base in range(0, faces, 256):
        pick[pl.ds(base, 256), :] = one_hot_rows(partner, base, 256)
    near[...] = mm(traces0, pick_near[...]) - traces0.astype(F32)
    grad_near[...] = mm_nt(jump0_b, pick_near[...]) - jump0

    def iota(shape, axis):
        return lax.broadcasted_iota(jnp.int32, shape, axis)

    def hot(mask):
        return jnp.where(mask, 1.0, 0.0).astype(BF)

    e1 = hot(iota((1024, 64), 0) % 64 == iota((1024, 64), 1))
    e1t = hot(iota((64, 1024), 1) % 64 == iota((64, 1024), 0))
    e2 = hot(iota((10, 160), 1) // 16 == iota((10, 160), 0))
    e2t = hot(iota((160, 10), 0) // 16 == iota((160, 10), 1))
    e3 = hot(iota((5, 80), 1) // 16 == iota((5, 80), 0))
    e3t = hot(iota((80, 5), 0) // 16 == iota((80, 5), 1))
    in_w, mid_w, out_w = in_w_ref[...], mid_w_ref[...], out_w_ref[...]

    def masked(values, mask):
        return jnp.where(mask, values, 0.0).astype(BF)

    w1[...] = masked(
        mm(mm(e1, in_w).astype(BF), e2),
        iota((1024, 160), 0) // 64 == iota((1024, 160), 1) % 16,
    )
    w1t[...] = masked(
        mm(mm_nt(e2t, in_w).astype(BF), e1t),
        iota((160, 1024), 1) // 64 == iota((160, 1024), 0) % 16,
    )
    o16[...] = masked(
        mm(mm(e3t, out_w).astype(BF), e1t),
        iota((80, 1024), 1) // 64 == iota((80, 1024), 0) % 16,
    )
    o16t[...] = masked(
        mm(mm_nt(e1, out_w).astype(BF), e3),
        iota((1024, 80), 0) // 64 == iota((1024, 80), 1) % 16,
    )
    same = iota((256, 256), 0) // 64 == iota((256, 256), 1) // 64
    m4[...] = masked(mm(mm(e1[:256], mid_w).astype(BF), e1t[:, :256]), same)
    m4t[...] = masked(mm(mm_nt(e1[:256], mid_w).astype(BF), e1t[:, :256]), same)
    diag = iota((256, 64), 0) % 64 == iota((256, 64), 1)
    for bias_ref, target in ((in_b_ref, bias1), (mid_b_ref, bias2)):
        column = jnp.sum(jnp.where(diag, bias_ref[...], 0.0), axis=1, keepdims=True)
        target[...] = jnp.broadcast_to(column, target.shape)

    def activations(x, sub):
        h1 = jnp.tanh(mm(w1[pl.ds(sub * 256, 256), :], x) + bias1[...])
        h2 = jnp.tanh(mm(m4[...], h1.astype(BF)) + bias2[...])
        return h1, h2

    def back(upstream, sub, factor1, factor2):
        d2 = (mm(o16t[pl.ds(sub * 256, 256), :], upstream) * factor2).astype(BF)
        d1 = (mm(m4t[...], d2) * factor1).astype(BF)
        return mm(w1t[:, pl.ds(sub * 256, 256)], d1)

    def nodes_of(g):
        return pl.ds(pl.multiple_of(g * 16, 16), 16)

    def set_inputs(field_b, volume_b):
        x_in[0:5] = field_b.reshape(5, 64, elements)
        x_in[5:10] = volume_b.reshape(5, 64, elements)

    volume0 = mm(vol_op_ref[...], field0)
    set_inputs(field0, volume0.astype(BF))

    def forward_group(g, carry):
        x = x_in[:, nodes_of(g), :].reshape(160, elements)
        total = jnp.zeros((80, elements), F32)
        for sub in range(4):
            h1, h2 = activations(x, sub)
            rows = pl.ds(pl.multiple_of(g * 1024 + sub * 256, 256), 256)
            slope1[rows, :] = (1.0 - h1 * h1).astype(BF)
            slope2[rows, :] = (1.0 - h2 * h2).astype(BF)
            total = total + mm(o16[:, pl.ds(sub * 256, 256)], h2.astype(BF))
        clo[:, nodes_of(g), :] = total.reshape(5, 16, elements)
        return carry

    lax.fori_loop(0, 4, forward_group, 0)
    base0 = w_ref[...] + time_step * (volume0 + clo[...].reshape(320, elements))

    wait_exchange(0)
    jump = near[...] + mm(got_forward(0), pick_far[...])
    flux = mix(flux_ref, lift_gain * jump, False)
    middle = base0 + time_step * lift(face_t, flux, elements)
    middle_s[...] = middle
    trace_grad = grad_near[...] + mm_nt(got_backward(0), send_hot[...])
    adj_lift = lift(face_t, trace_grad, elements)

    field1 = middle.astype(BF)
    traces1 = traces_of(field1)
    traces_s[...] = traces1
    put_forward(1, mm(traces1, send_hot[...]))
    volume1 = mm(vol_op_ref[...], field1)
    set_inputs(field1, volume1.astype(BF))
    g_in[...] = ct_ref[...].astype(BF).reshape(5, 64, elements)

    def both_group(g, carry):
        x = x_in[:, nodes_of(g), :].reshape(160, elements)
        upstream = g_in[:, nodes_of(g), :].reshape(80, elements)
        total = jnp.zeros((80, elements), F32)
        grads = jnp.zeros((160, elements), F32)
        for sub in range(4):
            h1, h2 = activations(x, sub)
            total = total + mm(o16[:, pl.ds(sub * 256, 256)], h2.astype(BF))
            grads = grads + back(upstream, sub, 1.0 - h1 * h1, 1.0 - h2 * h2)
        clo[:, nodes_of(g), :] = total.reshape(5, 16, elements)
        x_grad[:, nodes_of(g), :] = grads.reshape(10, 16, elements)
        return carry

    lax.fori_loop(0, 4, both_group, 0)

    def input_part(adjoint):
        field_grad = x_grad[0:5].reshape(320, elements)
        volume_grad = x_grad[5:10].reshape(320, elements)
        return mm_tn(vol_op_ref[...], (adjoint + volume_grad).astype(BF)) + field_grad

    ct = ct_ref[...]
    adj_mid = 0.5 * ct + 0.5 * time_step * (input_part(ct) + adj_lift)
    adj_mid_s[...] = adj_mid
    jump1 = jump_grad_of(adj_mid)
    jump1_b = jump1.astype(BF)
    put_backward(1, mm_nt(jump1_b, pick_far[...]))
    start_exchange(1)

    final_ref[...] = 0.5 * w_ref[...] + 0.5 * (
        middle_s[...] + time_step * (volume1 + clo[...].reshape(320, elements))
    )
    near[...] = mm(traces_s[...], pick_near[...]) - traces_s[...].astype(F32)
    grad_near[...] = mm_nt(jump1_b, pick_near[...]) - jump1
    g_in[...] = adj_mid.astype(BF).reshape(5, 64, elements)

    def back_group(g, carry):
        upstream = g_in[:, nodes_of(g), :].reshape(80, elements)
        grads = jnp.zeros((160, elements), F32)
        for sub in range(4):
            rows = pl.ds(pl.multiple_of(g * 1024 + sub * 256, 256), 256)
            grads = grads + back(
                upstream, sub, slope1[rows, :].astype(F32), slope2[rows, :].astype(F32)
            )
        x_grad[:, nodes_of(g), :] = grads.reshape(10, 16, elements)
        return carry

    lax.fori_loop(0, 4, back_group, 0)
    adj_mid = adj_mid_s[...]
    adj_ref[...] = 0.5 * ct_ref[...] + adj_mid + time_step * input_part(adj_mid)

    wait_exchange(1)
    jump = near[...] + mm(got_forward(1), pick_far[...])
    flux = mix(flux_ref, lift_gain * jump, False)
    final_ref[...] += 0.5 * time_step * lift(face_t, flux, elements)
    trace_grad = grad_near[...] + mm_nt(got_backward(1), send_hot[...])
    adj_ref[...] += time_step * lift(face_t, trace_grad, elements)


def body(
    n_dom,
    n_sub,
    initial_state,
    cotangent,
    volume_operator,
    in_weight,
    in_bias,
    mid_weight,
    mid_bias,
    out_weight,
    flux_matrix,
    dom_send,
    dom_count,
    sub_send,
    partner,
):
    elements = initial_state.shape[1]
    faces = 6 * elements
    slots = dom_send.shape[1] + sub_send.shape[1]
    table = face_rows()
    vmem = pl.BlockSpec(memory_space=pltpu.VMEM)
    smem = pl.BlockSpec(memory_space=pltpu.SMEM)
    state = jax.ShapeDtypeStruct(initial_state.shape, F32)
    return pl.pallas_call(
        functools.partial(kernel, n_dom, n_sub),
        out_shape=(state, state),
        in_specs=[vmem] * 8 + [smem, vmem, smem] + [vmem] * 4,
        out_specs=(vmem, vmem),
        scratch_shapes=[
            pltpu.VMEM((faces + slots, faces), BF),
            pltpu.VMEM((faces, slots), BF),
            pltpu.VMEM((1024, 160), BF),
            pltpu.VMEM((160, 1024), BF),
            pltpu.VMEM((256, 256), BF),
            pltpu.VMEM((256, 256), BF),
            pltpu.VMEM((80, 1024), BF),
            pltpu.VMEM((1024, 80), BF),
            pltpu.VMEM((256, elements), F32),
            pltpu.VMEM((256, elements), F32),
            pltpu.VMEM((10, 64, elements), BF),
            pltpu.VMEM((5, 64, elements), BF),
            pltpu.VMEM((5, 64, elements), F32),
            pltpu.VMEM((10, 64, elements), F32),
            pltpu.VMEM((4096, elements), BF),
            pltpu.VMEM((4096, elements), BF),
            pltpu.VMEM((80, faces), BF),
            pltpu.VMEM((80, faces), F32),
            pltpu.VMEM((80, faces), F32),
            pltpu.VMEM(initial_state.shape, F32),
            pltpu.VMEM(initial_state.shape, F32),
            pltpu.VMEM((2, slots, 256), BF),
            pltpu.VMEM((2, slots, 256), BF),
            pltpu.SemaphoreType.DMA((2, PAIRS)),
            pltpu.SemaphoreType.DMA((2, PAIRS)),
            pltpu.SemaphoreType.DMA((2, n_sub - 1)),
            pltpu.SemaphoreType.DMA((2, n_sub - 1)),
        ],
        compiler_params=pltpu.CompilerParams(
            collective_id=0, has_side_effects=True, vmem_limit_bytes=56 * 1024 * 1024
        ),
        cost_estimate=pl.CostEstimate(
            flops=8_000_000_000, bytes_accessed=4_000_000, transcendentals=4_000_000
        ),
    )(
        initial_state,
        cotangent,
        volume_operator,
        in_weight,
        in_bias.reshape(1, -1),
        mid_weight,
        mid_bias.reshape(1, -1),
        out_weight,
        flux_matrix,
        dom_send,
        dom_count,
        sub_send,
        partner,
        jnp.asarray(table, BF),
        jnp.asarray(table.T, BF),
    )


def solution(mesh):
    return jax.shard_map(
        functools.partial(body, mesh.shape["dom"], mesh.shape["sub"]),
        mesh=mesh,
        in_specs=(
            P(None, ("dom", "sub")),
            P(None, ("dom", "sub")),
            P(),
            P(),
            P(),
            P(),
            P(),
            P(),
            P(),
            P("dom", "sub"),
            P("dom", "sub"),
            P("dom", "sub"),
            P("dom", "sub"),
        ),
        out_specs=(P(None, ("dom", "sub")), P(None, ("dom", "sub"))),
        check_vma=False,
    )
```

profile of v0, /device:TPU:0, one launch (start us, length us, event | category | flops | bytes accessed | tf_op | source)
XLA Modules:
  0.0 42.8 jit_solution(17383766710991919922)
XLA Ops:
  0.6 1.4 %copy.17.in_w_ref = bf16[64,10]{1,0:T(8,128)(2,1)} copy(bf16[64,10]{0,1:T(8,128)(2,1)} %param.18) | data formatting | bytes 2560 | tf_op args[3]
  2.0 38.2 %shard_map.158 = (f32[320,256]{1,0:T(8,128)}, f32[320,256]{1,0:T(8,128)}) custom-call(f32[320,256]{1,0:T(8,128)} %w_ref.1, f32[320,256]{1,0:T(8,128)} %ct_ref.1, bf16[320,320]{1,0:T(8,128)(2,1)} %vol_op_ref.1, bf16[64,10]{1,0:T(8,128)(2,1)} %copy.17.in_w_ref, f32[1,64]{1,0:T(1,128)} %bitcast.2, bf16[64,64]{1,0:T(8,128)(2,1)} %mid_w_ref.1, f32[1,64]{1,0:T(1,128)} %bitcast.3, ...), custom_call_target="tpu_custom_call" | custom-call | flops 8000000000 | bytes 4000000 | tf_op jit(solution)/shard_map/pallas_call | solution.py:462
  40.2 0.0 copy-start
  40.3 1.8 %copy.20 = f32[320,256]{1,0:T(8,128)} copy(f32[320,256]{1,0:T(8,128)} %get-tuple-element.4) | data formatting | bytes 655360
  42.0 0.0 copy-done
  42.0 0.7 %copy.21 = f32[320,256]{1,0:T(8,128)} copy(f32[320,256]{1,0:T(8,128)S(1)} %copy-done) | data formatting | bytes 655360
Async XLA Ops:
  40.2 1.8 %copy-start = (f32[320,256]{1,0:T(8,128)S(1)}, f32[320,256]{1,0:T(8,128)}, u32[]{:S(2)}) copy-start(f32[320,256]{1,0:T(8,128)} %get-tuple-element.5) | copy-start | bytes 983044
where the time goes:
time: 42.9 us; the launch traced here: 42.8 us
  Pallas kernels  38.2 us (89%)
  local copies, waits for them, and re-layouts  3.88 us (9%)
  between operations  0.65 us (2%)
    pallas_call x1, Pallas kernels, body(): pl.pallas_call(functools.partial(kernel, n_dom, n_sub), out_shape=(state,...  38.2 us
    unnamed x5, local copies, waits for them, and re-layouts  3.88 us

commit v1 on v0

--- a/solution.py
+++ b/solution.py
@@ -2,7 +2,6 @@
 
 import jax
 import jax.numpy as jnp
-import numpy as np
 from jax import lax
 from jax.experimental import pallas as pl
 from jax.experimental.pallas import tpu as pltpu
@@ -19,22 +18,25 @@
 F32 = jnp.float32
 
 
-def face_rows():
-    table = np.zeros((6, 5, 16, 5, 64), np.float32)
-    for k in range(16):
-        low, high = k % 4, k // 4
-        nodes = [
-            4 * k,
-            3 + 4 * k,
-            low + 16 * high,
-            low + 12 + 16 * high,
-            k,
-            k + 48,
-        ]
-        for f, node in enumerate(nodes):
-            for v in range(5):
-                table[f, v, k, v, node] = 1.0
-    return table.reshape(480, 320)
+def iota(shape, axis):
+    return lax.broadcasted_iota(jnp.int32, shape, axis)
+
+
+def hot(mask):
+    return jnp.where(mask, 1.0, 0.0).astype(BF)
+
+
+def face_node(row):
+    f = sum((row >= 80 * i).astype(jnp.int32) for i in range(1, 6))
+    within = row - 80 * f
+    v, k = within >> 4, within & 15
+    end = f & 1
+    node = jnp.where(
+        f < 2,
+        3 * end + 4 * k,
+        jnp.where(f < 4, (k & 3) + 16 * (k >> 2) + 12 * end, k + 48 * end),
+    )
+    return 64 * v + node
 
 
 def mm(a, b):
@@ -95,7 +97,7 @@
     w_ref,
     ct_ref,
     vol_op_ref,
-    in_w_ref,
+    in_wt_ref,
     in_b_ref,
     mid_w_ref,
     mid_b_ref,
@@ -105,8 +107,6 @@
     count_ref,
     sub_ref,
     partner_ref,
-    face_ref,
-    face_t_ref,
     final_ref,
     adj_ref,
     pick,
@@ -128,6 +128,8 @@
     traces_s,
     near,
     grad_near,
+    jump0_s,
+    jump1_s,
     middle_s,
     adj_mid_s,
     out_buf,
@@ -228,22 +230,21 @@
         ]
         return jnp.concatenate(parts + [rows[dom_width:]], axis=0)
 
-    def slots_to_rows(values):
-        padded = jnp.concatenate([values, jnp.zeros((48, slots), F32)], axis=0)
-        return jnp.transpose(padded)
-
     def put_forward(phase, values):
-        out_buf[phase, :, 0:128] = slots_to_rows(values).astype(BF)
-
-    def put_backward(phase, values):
-        out_buf[phase, :, 128:256] = flip(slots_to_rows(values)).astype(BF)
+        out_buf[phase, :, 0:128] = to_rows(values).astype(BF)
+
+    def to_rows(values):
+        padding = jnp.zeros((48, values.shape[1]), F32)
+        return jnp.transpose(jnp.concatenate([values, padding], axis=0))
+
+    def put_backward(phase, rows):
+        out_buf[phase, :, 128:256] = flip(rows.astype(BF))
 
     def got_forward(phase):
         return jnp.transpose(in_buf[phase, :, 0:128].astype(F32))[:80].astype(BF)
 
     def got_backward(phase):
-        rows = flip(in_buf[phase, :, 128:256].astype(F32))
-        return jnp.transpose(rows)[:80].astype(BF)
+        return flip(in_buf[phase, :, 128:256])
 
     lane = lax.broadcasted_iota(jnp.int32, (1, dom_width), 1)
     dom_list = dom_ref[...]
@@ -257,8 +258,8 @@
     for base in range(faces, faces + slots, 256):
         pick[pl.ds(base, 256), :] = one_hot_rows(partner, base, 256)
 
-    face = face_ref[...]
-    face_t = face_t_ref[...]
+    face = hot(iota((480, 320), 1) == face_node(iota((480, 1), 0)))
+    face_t = hot(iota((320, 480), 0) == face_node(iota((1, 480), 1)))
 
     def traces_of(field_b):
         return to_wide(mm(face, field_b), elements).astype(BF)
@@ -275,53 +276,48 @@
     traces0 = traces_of(field0)
     put_forward(0, mm(traces0, send_hot[...]))
     jump0 = jump_grad_of(ct_ref[...])
-    jump0_b = jump0.astype(BF)
-    put_backward(0, mm_nt(jump0_b, pick_far[...]))
+    jump0_s[...] = jump0
+    jump0_rows = to_rows(jump0).astype(BF)
+    put_backward(0, mm(pick_far[...], jump0_rows))
     pl.semaphore_wait(barrier, expected)
     start_exchange(0)
 
     for base in range(0, faces, 256):
         pick[pl.ds(base, 256), :] = one_hot_rows(partner, base, 256)
     near[...] = mm(traces0, pick_near[...]) - traces0.astype(F32)
-    grad_near[...] = mm_nt(jump0_b, pick_near[...]) - jump0
-
-    def iota(shape, axis):
-        return lax.broadcasted_iota(jnp.int32, shape, axis)
-
-    def hot(mask):
-        return jnp.where(mask, 1.0, 0.0).astype(BF)
-
-    e1 = hot(iota((1024, 64), 0) % 64 == iota((1024, 64), 1))
-    e1t = hot(iota((64, 1024), 1) % 64 == iota((64, 1024), 0))
-    e2 = hot(iota((10, 160), 1) // 16 == iota((10, 160), 0))
-    e2t = hot(iota((160, 10), 0) // 16 == iota((160, 10), 1))
-    e3 = hot(iota((5, 80), 1) // 16 == iota((5, 80), 0))
-    e3t = hot(iota((80, 5), 0) // 16 == iota((80, 5), 1))
-    in_w, mid_w, out_w = in_w_ref[...], mid_w_ref[...], out_w_ref[...]
+    grad_near[...] = mm(pick_near[...], jump0_rows)
+
+    e1 = hot((iota((1024, 64), 0) & 63) == iota((1024, 64), 1))
+    e1t = hot((iota((64, 1024), 1) & 63) == iota((64, 1024), 0))
+    e2 = hot((iota((10, 160), 1) >> 4) == iota((10, 160), 0))
+    e2t = hot((iota((160, 10), 0) >> 4) == iota((160, 10), 1))
+    e3 = hot((iota((5, 80), 1) >> 4) == iota((5, 80), 0))
+    e3t = hot((iota((80, 5), 0) >> 4) == iota((80, 5), 1))
+    in_wt, mid_w, out_w = in_wt_ref[...], mid_w_ref[...], out_w_ref[...]
 
     def masked(values, mask):
         return jnp.where(mask, values, 0.0).astype(BF)
 
     w1[...] = masked(
-        mm(mm(e1, in_w).astype(BF), e2),
-        iota((1024, 160), 0) // 64 == iota((1024, 160), 1) % 16,
+        mm(mm_nt(e1, in_wt).astype(BF), e2),
+        (iota((1024, 160), 0) >> 6) == (iota((1024, 160), 1) & 15),
     )
     w1t[...] = masked(
-        mm(mm_nt(e2t, in_w).astype(BF), e1t),
-        iota((160, 1024), 1) // 64 == iota((160, 1024), 0) % 16,
+        mm(mm(e2t, in_wt).astype(BF), e1t),
+        (iota((160, 1024), 1) >> 6) == (iota((160, 1024), 0) & 15),
     )
     o16[...] = masked(
         mm(mm(e3t, out_w).astype(BF), e1t),
-        iota((80, 1024), 1) // 64 == iota((80, 1024), 0) % 16,
+        (iota((80, 1024), 1) >> 6) == (iota((80, 1024), 0) & 15),
     )
     o16t[...] = masked(
         mm(mm_nt(e1, out_w).astype(BF), e3),
-        iota((1024, 80), 0) // 64 == iota((1024, 80), 1) % 16,
-    )
-    same = iota((256, 256), 0) // 64 == iota((256, 256), 1) // 64
+        (iota((1024, 80), 0) >> 6) == (iota((1024, 80), 1) & 15),
+    )
+    same = (iota((256, 256), 0) >> 6) == (iota((256, 256), 1) >> 6)
     m4[...] = masked(mm(mm(e1[:256], mid_w).astype(BF), e1t[:, :256]), same)
     m4t[...] = masked(mm(mm_nt(e1[:256], mid_w).astype(BF), e1t[:, :256]), same)
-    diag = iota((256, 64), 0) % 64 == iota((256, 64), 1)
+    diag = (iota((256, 64), 0) & 63) == iota((256, 64), 1)
     for bias_ref, target in ((in_b_ref, bias1), (mid_b_ref, bias2)):
         column = jnp.sum(jnp.where(diag, bias_ref[...], 0.0), axis=1, keepdims=True)
         target[...] = jnp.broadcast_to(column, target.shape)
@@ -366,7 +362,8 @@
     flux = mix(flux_ref, lift_gain * jump, False)
     middle = base0 + time_step * lift(face_t, flux, elements)
     middle_s[...] = middle
-    trace_grad = grad_near[...] + mm_nt(got_backward(0), send_hot[...])
+    rows = grad_near[...] + mm(send_hot[...], got_backward(0))
+    trace_grad = jnp.transpose(rows)[:80] - jump0_s[...]
     adj_lift = lift(face_t, trace_grad, elements)
 
     field1 = middle.astype(BF)
@@ -401,15 +398,16 @@
     adj_mid = 0.5 * ct + 0.5 * time_step * (input_part(ct) + adj_lift)
     adj_mid_s[...] = adj_mid
     jump1 = jump_grad_of(adj_mid)
-    jump1_b = jump1.astype(BF)
-    put_backward(1, mm_nt(jump1_b, pick_far[...]))
+    jump1_s[...] = jump1
+    jump1_rows = to_rows(jump1).astype(BF)
+    put_backward(1, mm(pick_far[...], jump1_rows))
     start_exchange(1)
 
     final_ref[...] = 0.5 * w_ref[...] + 0.5 * (
         middle_s[...] + time_step * (volume1 + clo[...].reshape(320, elements))
     )
     near[...] = mm(traces_s[...], pick_near[...]) - traces_s[...].astype(F32)
-    grad_near[...] = mm_nt(jump1_b, pick_near[...]) - jump1
+    grad_near[...] = mm(pick_near[...], jump1_rows)
     g_in[...] = adj_mid.astype(BF).reshape(5, 64, elements)
 
     def back_group(g, carry):
@@ -431,7 +429,8 @@
     jump = near[...] + mm(got_forward(1), pick_far[...])
     flux = mix(flux_ref, lift_gain * jump, False)
     final_ref[...] += 0.5 * time_step * lift(face_t, flux, elements)
-    trace_grad = grad_near[...] + mm_nt(got_backward(1), send_hot[...])
+    rows = grad_near[...] + mm(send_hot[...], got_backward(1))
+    trace_grad = jnp.transpose(rows)[:80] - jump1_s[...]
     adj_ref[...] += time_step * lift(face_t, trace_grad, elements)
 
 
@@ -455,14 +454,13 @@
     elements = initial_state.shape[1]
     faces = 6 * elements
     slots = dom_send.shape[1] + sub_send.shape[1]
-    table = face_rows()
     vmem = pl.BlockSpec(memory_space=pltpu.VMEM)
     smem = pl.BlockSpec(memory_space=pltpu.SMEM)
     state = jax.ShapeDtypeStruct(initial_state.shape, F32)
     return pl.pallas_call(
         functools.partial(kernel, n_dom, n_sub),
         out_shape=(state, state),
-        in_specs=[vmem] * 8 + [smem, vmem, smem] + [vmem] * 4,
+        in_specs=[vmem] * 8 + [smem, vmem, smem] + [vmem] * 2,
         out_specs=(vmem, vmem),
         scratch_shapes=[
             pltpu.VMEM((faces + slots, faces), BF),
@@ -483,6 +481,8 @@
             pltpu.VMEM((4096, elements), BF),
             pltpu.VMEM((80, faces), BF),
             pltpu.VMEM((80, faces), F32),
+            pltpu.VMEM((faces, 128), F32),
+            pltpu.VMEM((80, faces), F32),
             pltpu.VMEM((80, faces), F32),
             pltpu.VMEM(initial_state.shape, F32),
             pltpu.VMEM(initial_state.shape, F32),
@@ -494,7 +494,7 @@
             pltpu.SemaphoreType.DMA((2, n_sub - 1)),
         ],
         compiler_params=pltpu.CompilerParams(
-            collective_id=0, has_side_effects=True, vmem_limit_bytes=56 * 1024 * 1024
+            collective_id=0, has_side_effects=True, vmem_limit_bytes=32 * 1024 * 1024
         ),
         cost_estimate=pl.CostEstimate(
             flops=8_000_000_000, bytes_accessed=4_000_000, transcendentals=4_000_000
@@ -503,7 +503,7 @@
         initial_state,
         cotangent,
         volume_operator,
-        in_weight,
+        in_weight.T,
         in_bias.reshape(1, -1),
         mid_weight,
         mid_bias.reshape(1, -1),
@@ -513,8 +513,6 @@
         dom_count,
         sub_send,
         partner,
-        jnp.asarray(table, BF),
-        jnp.asarray(table.T, BF),
     )
 
 

time: 42.9 us -> 48.3 us (1.13)
  local copies, waits for them, and re-layouts: 3.88 us -> 9.78 us
  Pallas kernels: 38.2 us -> 37.4 us
    unnamed x5 -> x28, local copies, waits for them, and re-layouts: 3.88 us -> 9.78 us
    pallas_call x1, Pallas kernels: 38.2 us -> 37.4 us  [body(): pl.pallas_call(functools.partial(kernel, n_dom, n_sub), out_shape=(state,...]
where the time goes in v1:
time: 48.3 us; the launch traced here: 47.8 us
  Pallas kernels  37.4 us (77%)
  local copies, waits for them, and re-layouts  9.78 us (20%)
  between operations  0.68 us (1%)
    pallas_call x1, Pallas kernels, body(): pl.pallas_call(functools.partial(kernel, n_dom, n_sub), out_shape=(state,...  37.4 us
    unnamed x28, local copies, waits for them, and re-layouts  9.78 us

profile of v1, /device:TPU:0, one launch (start us, length us, event | category | flops | bytes accessed | tf_op | source)
XLA Modules:
  0.0 47.8 jit_solution(1586049028938250057)
XLA Ops:
  0.6 0.0 copy-start.5
  0.6 0.0 copy-start.9
  0.7 0.0 copy-start.10
  0.7 0.7 %copy-done.5 = bf16[64,10]{0,1:T(8,128)(2,1)S(1)} copy-done((bf16[64,10]{0,1:T(8,128)(2,1)S(1)}, bf16[64,10]{0,1:T(8,128)(2,1)}, u32[]{:S(2)}) %copy-start.5) | copy-done | bytes 1304
  1.3 0.0 copy-done.9
  1.3 0.0 copy-done.10
  1.3 0.0 copy-start
  1.3 1.0 %copy-done = f32[320,256]{1,0:T(8,128)S(1)} copy-done((f32[320,256]{1,0:T(8,128)S(1)}, f32[320,256]{1,0:T(8,128)}, u32[]{:S(2)}) %copy-start) | copy-done | bytes 327704
  2.3 0.0 copy-start.1
  2.3 1.0 %copy-done.1 = f32[320,256]{1,0:T(8,128)S(1)} copy-done((f32[320,256]{1,0:T(8,128)S(1)}, f32[320,256]{1,0:T(8,128)}, u32[]{:S(2)}) %copy-start.1) | copy-done | bytes 327704
  3.3 0.0 copy-start.2
  3.3 0.9 %copy-done.2 = bf16[320,320]{1,0:T(8,128)(2,1)S(1)} copy-done((bf16[320,320]{1,0:T(8,128)(2,1)S(1)}, bf16[320,320]{1,0:T(8,128)(2,1)}, u32[]{:S(2)}) %copy-start.2) | copy-done | bytes 204824
  4.2 0.0 copy-start.3
  4.2 0.7 %copy-done.3 = bf16[64,64]{1,0:T(8,128)(2,1)S(1)} copy-done((bf16[64,64]{1,0:T(8,128)(2,1)S(1)}, bf16[64,64]{1,0:T(8,128)(2,1)}, u32[]{:S(2)}) %copy-start.3) | copy-done | bytes 8216
  4.9 0.0 copy-start.4
  4.9 0.7 %copy-done.4 = s32[1,1536]{1,0:T(1,128)S(1)} copy-done((s32[1,1536]{1,0:T(1,128)S(1)}, s32[1,1536]{1,0:T(1,128)}, u32[]{:S(2)}) %copy-start.4) | copy-done | bytes 6168
  5.6 0.7 %copy-done.6 = f32[5,5]{1,0:T(8,128)S(1)} copy-done((f32[5,5]{1,0:T(8,128)S(1)}, f32[5,5]{1,0:T(8,128)}, u32[]{:S(2)}) %copy-start.6) | copy-done | bytes 124
  6.3 0.7 %copy-done.7 = bf16[5,64]{1,0:T(8,128)(2,1)S(1)} copy-done((bf16[5,64]{1,0:T(8,128)(2,1)S(1)}, bf16[5,64]{1,0:T(8,128)(2,1)}, u32[]{:S(2)}) %copy-start.7) | copy-done | bytes 664
  7.0 0.7 %copy-done.8 = s32[1,512]{1,0:T(1,128)S(1)} copy-done((s32[1,512]{1,0:T(1,128)S(1)}, s32[1,512]{1,0:T(1,128)}, u32[]{:S(2)}) %copy-start.8) | copy-done | bytes 2072
  7.7 0.7 %copy-done.11 = f32[64]{0:T(128)S(1)} copy-done((f32[64]{0:T(128)S(1)}, f32[64]{0:T(128)}, u32[]{:S(2)}) %copy-start.11) | copy-done | bytes 280
  8.3 0.7 %copy-done.12 = s32[1,8]{1,0:T(1,128)S(1)} copy-done((s32[1,8]{1,0:T(1,128)S(1)}, s32[1,8]{1,0:T(1,128)}, u32[]{:S(2)}) %copy-start.12) | copy-done | bytes 56
  9.0 37.4 %shard_map.140 = (f32[320,256]{1,0:T(8,128)S(1)}, f32[320,256]{1,0:T(8,128)S(1)}) custom-call(f32[320,256]{1,0:T(8,128)S(1)} %copy-done, f32[320,256]{1,0:T(8,128)S(1)} %copy-done.1, bf16[320,320]{1,0:T(8,128)(2,1)S(1)} %copy-done.2, bf16[10,64]{1,0:T(8,128)(2,1)S(1)} %bitcast.3, f32[1,64]{1,0:T(1,128)S(1)} %bitcast.4, bf16[64,64]{1,0:T(8,128)(2,1)S(1)} %copy-done.3, ...), custom_call_target="tpu_custom_call" | custom-call | flops 8000000000 | bytes 4000000 | tf_op jit(solution)/shard_map/pallas_call | solution.py:460
  46.4 0.7 %copy.17 = f32[320,256]{1,0:T(8,128)} copy(f32[320,256]{1,0:T(8,128)S(1)} %get-tuple-element.4) | data formatting | bytes 655360
  47.1 0.7 %copy.18 = f32[320,256]{1,0:T(8,128)} copy(f32[320,256]{1,0:T(8,128)S(1)} %get-tuple-element.5) | data formatting | bytes 655360
  (5 shorter events, 0.0 us)
Async XLA Ops:
  0.6 0.7 %copy-start.5 = (bf16[64,10]{0,1:T(8,128)(2,1)S(1)}, bf16[64,10]{0,1:T(8,128)(2,1)}, u32[]{:S(2)}) copy-start(bf16[64,10]{0,1:T(8,128)(2,1)} %param.16) | copy-start | bytes 3844
  0.6 0.7 %copy-start.9 = (s32[1,256]{1,0:T(1,128)S(1)}, s32[1,256]{1,0:T(1,128)}, u32[]{:S(2)}) copy-start(s32[1,256]{1,0:T(1,128)} %dom_ref.1) | copy-start | bytes 3076
  0.7 0.7 %copy-start.10 = (f32[64]{0:T(128)S(1)}, f32[64]{0:T(128)}, u32[]{:S(2)}) copy-start(f32[64]{0:T(128)} %param.17) | copy-start | bytes 772
  1.3 1.0 %copy-start = (f32[320,256]{1,0:T(8,128)S(1)}, f32[320,256]{1,0:T(8,128)}, u32[]{:S(2)}) copy-start(f32[320,256]{1,0:T(8,128)} %w_ref.1) | copy-start | bytes 983044
  2.3 1.0 %copy-start.1 = (f32[320,256]{1,0:T(8,128)S(1)}, f32[320,256]{1,0:T(8,128)}, u32[]{:S(2)}) copy-start(f32[320,256]{1,0:T(8,128)} %ct_ref.1) | copy-start | bytes 983044
  3.3 0.9 %copy-start.2 = (bf16[320,320]{1,0:T(8,128)(2,1)S(1)}, bf16[320,320]{1,0:T(8,128)(2,1)}, u32[]{:S(2)}) copy-start(bf16[320,320]{1,0:T(8,128)(2,1)} %vol_op_ref.1) | copy-start | bytes 614404
  4.2 0.7 %copy-start.3 = (bf16[64,64]{1,0:T(8,128)(2,1)S(1)}, bf16[64,64]{1,0:T(8,128)(2,1)}, u32[]{:S(2)}) copy-start(bf16[64,64]{1,0:T(8,128)(2,1)} %mid_w_ref.1) | copy-start | bytes 24580
  4.9 0.7 %copy-start.4 = (s32[1,1536]{1,0:T(1,128)S(1)}, s32[1,1536]{1,0:T(1,128)}, u32[]{:S(2)}) copy-start(s32[1,1536]{1,0:T(1,128)} %partner_ref.1) | copy-start | bytes 18436
  5.6 0.7 %copy-start.6 = (f32[5,5]{1,0:T(8,128)S(1)}, f32[5,5]{1,0:T(8,128)}, u32[]{:S(2)}) copy-start(f32[5,5]{1,0:T(8,128)} %flux_ref.1) | copy-start | bytes 304
  6.3 0.7 %copy-start.7 = (bf16[5,64]{1,0:T(8,128)(2,1)S(1)}, bf16[5,64]{1,0:T(8,128)(2,1)}, u32[]{:S(2)}) copy-start(bf16[5,64]{1,0:T(8,128)(2,1)} %out_w_ref.1) | copy-start | bytes 1924
  7.0 0.7 %copy-start.8 = (s32[1,512]{1,0:T(1,128)S(1)}, s32[1,512]{1,0:T(1,128)}, u32[]{:S(2)}) copy-start(s32[1,512]{1,0:T(1,128)} %sub_ref.1) | copy-start | bytes 6148
  7.7 0.7 %copy-start.11 = (f32[64]{0:T(128)S(1)}, f32[64]{0:T(128)}, u32[]{:S(2)}) copy-start(f32[64]{0:T(128)} %param.19) | copy-start | bytes 772
  8.3 0.7 %copy-start.12 = (s32[1,8]{1,0:T(1,128)S(1)}, s32[1,8]{1,0:T(1,128)}, u32[]{:S(2)}) copy-start(s32[1,8]{1,0:T(1,128)} %count_ref.1) | copy-start | bytes 100

commit v2 on v1

--- a/solution.py
+++ b/solution.py
@@ -117,8 +117,6 @@
     m4t,
     o16,
     o16t,
-    bias1,
-    bias2,
     x_in,
     g_in,
     clo,
@@ -289,73 +287,73 @@
 
     e1 = hot((iota((1024, 64), 0) & 63) == iota((1024, 64), 1))
     e1t = hot((iota((64, 1024), 1) & 63) == iota((64, 1024), 0))
-    e2 = hot((iota((10, 160), 1) >> 4) == iota((10, 160), 0))
-    e2t = hot((iota((160, 10), 0) >> 4) == iota((160, 10), 1))
-    e3 = hot((iota((5, 80), 1) >> 4) == iota((5, 80), 0))
-    e3t = hot((iota((80, 5), 0) >> 4) == iota((80, 5), 1))
+    e2 = hot((iota((10, 256), 1) >> 4) == iota((10, 256), 0))
+    e2t = hot((iota((256, 10), 0) >> 4) == iota((256, 10), 1))
+    e3 = hot((iota((5, 128), 1) >> 4) == iota((5, 128), 0))
+    e3t = hot((iota((128, 5), 0) >> 4) == iota((128, 5), 1))
     in_wt, mid_w, out_w = in_wt_ref[...], mid_w_ref[...], out_w_ref[...]
 
     def masked(values, mask):
         return jnp.where(mask, values, 0.0).astype(BF)
 
-    w1[...] = masked(
-        mm(mm_nt(e1, in_wt).astype(BF), e2),
-        (iota((1024, 160), 0) >> 6) == (iota((1024, 160), 1) & 15),
-    )
-    w1t[...] = masked(
-        mm(mm(e2t, in_wt).astype(BF), e1t),
-        (iota((160, 1024), 1) >> 6) == (iota((160, 1024), 0) & 15),
-    )
-    o16[...] = masked(
-        mm(mm(e3t, out_w).astype(BF), e1t),
-        (iota((80, 1024), 1) >> 6) == (iota((80, 1024), 0) & 15),
-    )
-    o16t[...] = masked(
-        mm(mm_nt(e1, out_w).astype(BF), e3),
-        (iota((1024, 80), 0) >> 6) == (iota((1024, 80), 1) & 15),
-    )
+    def node_match(shape, hidden_axis):
+        hidden = iota(shape, hidden_axis) >> 6
+        return hidden == (iota(shape, 1 - hidden_axis) & 15)
+
+    w1[...] = masked(mm(mm_nt(e1, in_wt).astype(BF), e2), node_match((1024, 256), 0))
+    w1t[...] = masked(mm(mm(e2t, in_wt).astype(BF), e1t), node_match((256, 1024), 1))
+    o16[...] = masked(mm(mm(e3t, out_w).astype(BF), e1t), node_match((128, 1024), 1))
+    o16t[...] = masked(mm(mm_nt(e1, out_w).astype(BF), e3), node_match((1024, 128), 0))
     same = (iota((256, 256), 0) >> 6) == (iota((256, 256), 1) >> 6)
     m4[...] = masked(mm(mm(e1[:256], mid_w).astype(BF), e1t[:, :256]), same)
     m4t[...] = masked(mm(mm_nt(e1[:256], mid_w).astype(BF), e1t[:, :256]), same)
-    diag = (iota((256, 64), 0) & 63) == iota((256, 64), 1)
-    for bias_ref, target in ((in_b_ref, bias1), (mid_b_ref, bias2)):
-        column = jnp.sum(jnp.where(diag, bias_ref[...], 0.0), axis=1, keepdims=True)
-        target[...] = jnp.broadcast_to(column, target.shape)
-
-    def activations(x, sub):
-        h1 = jnp.tanh(mm(w1[pl.ds(sub * 256, 256), :], x) + bias1[...])
-        h2 = jnp.tanh(mm(m4[...], h1.astype(BF)) + bias2[...])
+    bias1 = jnp.concatenate([in_b_ref[...]] * 4, axis=1)
+    bias2 = jnp.concatenate([mid_b_ref[...]] * 4, axis=1)
+
+    def group_rows(parts, width):
+        blocks = []
+        for g in range(4):
+            picked = [
+                part.reshape(5, 64, elements)[:, 16 * g : 16 * g + 16].reshape(80, elements)
+                for part in parts
+            ]
+            padding = jnp.zeros((width - 80 * len(parts), elements), F32)
+            blocks.append(jnp.transpose(jnp.concatenate(picked + [padding], axis=0)))
+        return jnp.concatenate(blocks, axis=0).astype(BF)
+
+    def ungroup(rows_ref, part):
+        blocks = []
+        for g in range(4):
+            block = jnp.transpose(rows_ref[pl.ds(g * elements, elements), :])
+            blocks.append(block[80 * part : 80 * part + 80].reshape(5, 16, elements))
+        return jnp.concatenate(blocks, axis=1).reshape(320, elements)
+
+    def columns_of(sub):
+        return pl.ds(pl.multiple_of(sub * 256, 256), 256)
+
+    def activations(sub):
+        h1 = jnp.tanh(mm(x_in[...], w1t[:, columns_of(sub)]) + bias1)
+        h2 = jnp.tanh(mm(h1.astype(BF), m4t[...]) + bias2)
         return h1, h2
 
-    def back(upstream, sub, factor1, factor2):
-        d2 = (mm(o16t[pl.ds(sub * 256, 256), :], upstream) * factor2).astype(BF)
-        d1 = (mm(m4t[...], d2) * factor1).astype(BF)
-        return mm(w1t[:, pl.ds(sub * 256, 256)], d1)
-
-    def nodes_of(g):
-        return pl.ds(pl.multiple_of(g * 16, 16), 16)
-
-    def set_inputs(field_b, volume_b):
-        x_in[0:5] = field_b.reshape(5, 64, elements)
-        x_in[5:10] = volume_b.reshape(5, 64, elements)
+    def back(sub, factor1, factor2):
+        d2 = (mm(g_in[...], o16[:, columns_of(sub)]) * factor2).astype(BF)
+        d1 = (mm(d2, m4[...]) * factor1).astype(BF)
+        x_grad[...] += mm(d1, w1[columns_of(sub), :])
 
     volume0 = mm(vol_op_ref[...], field0)
-    set_inputs(field0, volume0.astype(BF))
-
-    def forward_group(g, carry):
-        x = x_in[:, nodes_of(g), :].reshape(160, elements)
-        total = jnp.zeros((80, elements), F32)
-        for sub in range(4):
-            h1, h2 = activations(x, sub)
-            rows = pl.ds(pl.multiple_of(g * 1024 + sub * 256, 256), 256)
-            slope1[rows, :] = (1.0 - h1 * h1).astype(BF)
-            slope2[rows, :] = (1.0 - h2 * h2).astype(BF)
-            total = total + mm(o16[:, pl.ds(sub * 256, 256)], h2.astype(BF))
-        clo[:, nodes_of(g), :] = total.reshape(5, 16, elements)
+    x_in[...] = group_rows([field0.astype(F32), volume0], 256)
+    clo[...] = jnp.zeros_like(clo)
+
+    def forward_step(sub, carry):
+        h1, h2 = activations(sub)
+        slope1[sub] = (1.0 - h1 * h1).astype(BF)
+        slope2[sub] = (1.0 - h2 * h2).astype(BF)
+        clo[...] += mm(h2.astype(BF), o16t[columns_of(sub), :])
         return carry
 
-    lax.fori_loop(0, 4, forward_group, 0)
-    base0 = w_ref[...] + time_step * (volume0 + clo[...].reshape(320, elements))
+    lax.fori_loop(0, 4, forward_step, 0)
+    base0 = w_ref[...] + time_step * (volume0 + ungroup(clo, 0))
 
     wait_exchange(0)
     jump = near[...] + mm(got_forward(0), pick_far[...])
@@ -371,27 +369,21 @@
     traces_s[...] = traces1
     put_forward(1, mm(traces1, send_hot[...]))
     volume1 = mm(vol_op_ref[...], field1)
-    set_inputs(field1, volume1.astype(BF))
-    g_in[...] = ct_ref[...].astype(BF).reshape(5, 64, elements)
-
-    def both_group(g, carry):
-        x = x_in[:, nodes_of(g), :].reshape(160, elements)
-        upstream = g_in[:, nodes_of(g), :].reshape(80, elements)
-        total = jnp.zeros((80, elements), F32)
-        grads = jnp.zeros((160, elements), F32)
-        for sub in range(4):
-            h1, h2 = activations(x, sub)
-            total = total + mm(o16[:, pl.ds(sub * 256, 256)], h2.astype(BF))
-            grads = grads + back(upstream, sub, 1.0 - h1 * h1, 1.0 - h2 * h2)
-        clo[:, nodes_of(g), :] = total.reshape(5, 16, elements)
-        x_grad[:, nodes_of(g), :] = grads.reshape(10, 16, elements)
+    x_in[...] = group_rows([field1.astype(F32), volume1], 256)
+    g_in[...] = group_rows([ct_ref[...]], 128)
+    clo[...] = jnp.zeros_like(clo)
+    x_grad[...] = jnp.zeros_like(x_grad)
+
+    def both_step(sub, carry):
+        h1, h2 = activations(sub)
+        clo[...] += mm(h2.astype(BF), o16t[columns_of(sub), :])
+        back(sub, 1.0 - h1 * h1, 1.0 - h2 * h2)
         return carry
 
-    lax.fori_loop(0, 4, both_group, 0)
+    lax.fori_loop(0, 4, both_step, 0)
 
     def input_part(adjoint):
-        field_grad = x_grad[0:5].reshape(320, elements)
-        volume_grad = x_grad[5:10].reshape(320, elements)
+        field_grad, volume_grad = ungroup(x_grad, 0), ungroup(x_grad, 1)
         return mm_tn(vol_op_ref[...], (adjoint + volume_grad).astype(BF)) + field_grad
 
     ct = ct_ref[...]
@@ -404,24 +396,18 @@
     start_exchange(1)
 
     final_ref[...] = 0.5 * w_ref[...] + 0.5 * (
-        middle_s[...] + time_step * (volume1 + clo[...].reshape(320, elements))
+        middle_s[...] + time_step * (volume1 + ungroup(clo, 0))
     )
     near[...] = mm(traces_s[...], pick_near[...]) - traces_s[...].astype(F32)
     grad_near[...] = mm(pick_near[...], jump1_rows)
-    g_in[...] = adj_mid.astype(BF).reshape(5, 64, elements)
-
-    def back_group(g, carry):
-        upstream = g_in[:, nodes_of(g), :].reshape(80, elements)
-        grads = jnp.zeros((160, elements), F32)
-        for sub in range(4):
-            rows = pl.ds(pl.multiple_of(g * 1024 + sub * 256, 256), 256)
-            grads = grads + back(
-                upstream, sub, slope1[rows, :].astype(F32), slope2[rows, :].astype(F32)
-            )
-        x_grad[:, nodes_of(g), :] = grads.reshape(10, 16, elements)
+    g_in[...] = group_rows([adj_mid], 128)
+    x_grad[...] = jnp.zeros_like(x_grad)
+
+    def back_step(sub, carry):
+        back(sub, slope1[sub].astype(F32), slope2[sub].astype(F32))
         return carry
 
-    lax.fori_loop(0, 4, back_group, 0)
+    lax.fori_loop(0, 4, back_step, 0)
     adj_mid = adj_mid_s[...]
     adj_ref[...] = 0.5 * ct_ref[...] + adj_mid + time_step * input_part(adj_mid)
 
@@ -465,20 +451,18 @@
         scratch_shapes=[
             pltpu.VMEM((faces + slots, faces), BF),
             pltpu.VMEM((faces, slots), BF),
-            pltpu.VMEM((1024, 160), BF),
-            pltpu.VMEM((160, 1024), BF),
+            pltpu.VMEM((1024, 256), BF),
+            pltpu.VMEM((256, 1024), BF),
             pltpu.VMEM((256, 256), BF),
             pltpu.VMEM((256, 256), BF),
-            pltpu.VMEM((80, 1024), BF),
-            pltpu.VMEM((1024, 80), BF),
-            pltpu.VMEM((256, elements), F32),
-            pltpu.VMEM((256, elements), F32),
-            pltpu.VMEM((10, 64, elements), BF),
-            pltpu.VMEM((5, 64, elements), BF),
-            pltpu.VMEM((5, 64, elements), F32),
-            pltpu.VMEM((10, 64, elements), F32),
-            pltpu.VMEM((4096, elements), BF),
-            pltpu.VMEM((4096, elements), BF),
+            pltpu.VMEM((128, 1024), BF),
+            pltpu.VMEM((1024, 128), BF),
+            pltpu.VMEM((4 * elements, 256), BF),
+            pltpu.VMEM((4 * elements, 128), BF),
+            pltpu.VMEM((4 * elements, 128), F32),
+            pltpu.VMEM((4 * elements, 256), F32),
+            pltpu.VMEM((4, 4 * elements, 256), BF),
+            pltpu.VMEM((4, 4 * elements, 256), BF),
             pltpu.VMEM((80, faces), BF),
             pltpu.VMEM((80, faces), F32),
             pltpu.VMEM((faces, 128), F32),
@@ -494,7 +478,7 @@
             pltpu.SemaphoreType.DMA((2, n_sub - 1)),
         ],
         compiler_params=pltpu.CompilerParams(
-            collective_id=0, has_side_effects=True, vmem_limit_bytes=32 * 1024 * 1024
+            collective_id=0, has_side_effects=True, vmem_limit_bytes=56 * 1024 * 1024
         ),
         cost_estimate=pl.CostEstimate(
             flops=8_000_000_000, bytes_accessed=4_000_000, transcendentals=4_000_000

time: 48.3 us -> 35 us (0.72)
  local copies, waits for them, and re-layouts: 9.78 us -> 2.49 us
  Pallas kernels: 37.4 us -> 31.7 us
    unnamed x28 -> x4, local copies, waits for them, and re-layouts: 9.78 us -> 2.49 us
    pallas_call x1, Pallas kernels: 37.4 us -> 31.7 us  [body(): pl.pallas_call(functools.partial(kernel, n_dom, n_sub), out_shape=(state,...]
where the time goes in v2:
time: 35 us; the launch traced here: 34.8 us
  Pallas kernels  31.7 us (91%)
  local copies, waits for them, and re-layouts  2.49 us (7%)
  between operations  0.65 us (2%)
    pallas_call x1, Pallas kernels, body(): pl.pallas_call(functools.partial(kernel, n_dom, n_sub), out_shape=(state,...  31.7 us
    unnamed x4, local copies, waits for them, and re-layouts  2.49 us

profile of v2, /device:TPU:0, one launch (start us, length us, event | category | flops | bytes accessed | tf_op | source)
XLA Modules:
  0.0 34.8 jit_solution(17112185228289512606)
XLA Ops:
  0.6 31.7 %shard_map.140 = (f32[320,256]{1,0:T(8,128)}, f32[320,256]{1,0:T(8,128)}) custom-call(f32[320,256]{1,0:T(8,128)} %w_ref.1, f32[320,256]{1,0:T(8,128)} %ct_ref.1, bf16[320,320]{1,0:T(8,128)(2,1)} %vol_op_ref.1, bf16[10,64]{1,0:T(8,128)(2,1)} %bitcast.3, f32[1,64]{1,0:T(1,128)} %bitcast.4, bf16[64,64]{1,0:T(8,128)(2,1)} %mid_w_ref.1, f32[1,64]{1,0:T(1,128)} %bitcast.5, ...), custom_call_target="tpu_custom_call" | custom-call | flops 8000000000 | bytes 4000000 | tf_op jit(solution)/shard_map/pallas_call | solution.py:446
  32.3 0.0 copy-start
  32.3 1.8 %copy.17 = f32[320,256]{1,0:T(8,128)} copy(f32[320,256]{1,0:T(8,128)} %get-tuple-element.4) | data formatting | bytes 655360
  34.1 0.0 copy-done
  34.1 0.7 %copy.18 = f32[320,256]{1,0:T(8,128)} copy(f32[320,256]{1,0:T(8,128)S(1)} %copy-done) | data formatting | bytes 655360
Async XLA Ops:
  32.3 1.8 %copy-start = (f32[320,256]{1,0:T(8,128)S(1)}, f32[320,256]{1,0:T(8,128)}, u32[]{:S(2)}) copy-start(f32[320,256]{1,0:T(8,128)} %get-tuple-element.5) | copy-start | bytes 983044

commit v3 on v2

--- a/solution.py
+++ b/solution.py
@@ -66,8 +66,8 @@
     )
 
 
-def lift(face_t, wide, elements):
-    high, low = split(to_tall(wide, elements))
+def lift(face_t, tall):
+    high, low = split(tall)
     return mm(face_t, high) + mm(face_t, low)
 
 
@@ -83,12 +83,29 @@
     return jnp.concatenate(rows, axis=0)
 
 
-def one_hot_rows(row_list, base, rows):
+def one_hot_lanes(row_list):
     width = row_list.shape[1]
-    shifted = (row_list - base).astype(F32)
-    wide = jnp.broadcast_to(shifted, (rows, width))
-    spot = lax.broadcasted_iota(jnp.int32, (rows, width), 0).astype(F32)
-    return jnp.where(wide == spot, 1.0, 0.0).astype(BF)
+    low = jnp.broadcast_to(row_list & 255, (256, width))
+    return jnp.where(low == iota((256, width), 0), 1.0, 0.0)
+
+
+def pick_columns(blocks, low_hot, high, first):
+    picked = []
+    for base in range(0, high.shape[1], 256):
+        products = mm(blocks, low_hot[:, base : base + 256])
+        mine = high[:, base : base + 256]
+        total = jnp.zeros((80, 256), F32)
+        for b in range(blocks.shape[0] // 80):
+            total = jnp.where(mine == first + b, products[b * 80 : (b + 1) * 80], total)
+        picked.append(total)
+    return jnp.concatenate(picked, axis=1)
+
+
+def add_columns(values, low_hot_t, high, first, count):
+    parts = [
+        values * jnp.where(high == first + b, 1.0, 0.0).astype(BF) for b in range(count)
+    ]
+    return mm(jnp.concatenate(parts, axis=0), low_hot_t[...])
 
 
 def kernel(
@@ -109,8 +126,10 @@
     partner_ref,
     final_ref,
     adj_ref,
-    pick,
+    link_hot,
+    link_hot_t,
     send_hot,
+    send_hot_t,
     w1,
     w1t,
     m4,
@@ -126,8 +145,6 @@
     traces_s,
     near,
     grad_near,
-    jump0_s,
-    jump1_s,
     middle_s,
     adj_mid_s,
     out_buf,
@@ -235,14 +252,19 @@
         padding = jnp.zeros((48, values.shape[1]), F32)
         return jnp.transpose(jnp.concatenate([values, padding], axis=0))
 
-    def put_backward(phase, rows):
-        out_buf[phase, :, 128:256] = flip(rows.astype(BF))
+    def put_backward(phase, blocks):
+        wide = jnp.concatenate(
+            [blocks[80 * b : 80 * b + 80] for b in range(slots // 256)], axis=1
+        )
+        out_buf[phase, :, 128:256] = flip(to_rows(wide)).astype(BF)
 
     def got_forward(phase):
-        return jnp.transpose(in_buf[phase, :, 0:128].astype(F32))[:80].astype(BF)
+        wide = jnp.transpose(in_buf[phase, :, 0:128].astype(F32))[:80].astype(BF)
+        return jnp.concatenate([wide[:, b : b + 256] for b in range(0, slots, 256)], axis=0)
 
     def got_backward(phase):
-        return flip(in_buf[phase, :, 128:256])
+        rows = flip(in_buf[phase, :, 128:256].astype(F32))
+        return jnp.transpose(rows)[:80].astype(BF)
 
     lane = lax.broadcasted_iota(jnp.int32, (1, dom_width), 1)
     dom_list = dom_ref[...]
@@ -250,40 +272,43 @@
         dead = (lane >= j * peer_slots + count_ref[0, j]) & (lane < (j + 1) * peer_slots)
         dom_list = jnp.where(dead, -1, dom_list)
     send_list = jnp.concatenate([dom_list, sub_ref[...]], axis=1)
-    for base in range(0, faces, 256):
-        send_hot[pl.ds(base, 256), :] = one_hot_rows(send_list, base, 256)
+    send_low = one_hot_lanes(send_list)
+    send_hot[...] = send_low.astype(BF)
+    send_hot_t[...] = jnp.transpose(send_low).astype(BF)
+    send_high = send_list >> 8
     partner = partner_ref[...]
-    for base in range(faces, faces + slots, 256):
-        pick[pl.ds(base, 256), :] = one_hot_rows(partner, base, 256)
+    link_low = one_hot_lanes(partner)
+    link_hot[...] = link_low.astype(BF)
+    link_hot_t[...] = jnp.transpose(link_low).astype(BF)
+    link_high = partner >> 8
+    far_count = slots // 256
 
     face = hot(iota((480, 320), 1) == face_node(iota((480, 1), 0)))
     face_t = hot(iota((320, 480), 0) == face_node(iota((1, 480), 1)))
 
     def traces_of(field_b):
-        return to_wide(mm(face, field_b), elements).astype(BF)
+        return mm(face, field_b).astype(BF)
 
     def jump_grad_of(g):
         high, low = split(g)
         values = to_wide(mm(face, high) + mm(face, low), elements)
         return mix(flux_ref, lift_gain * values, True)
 
-    pick_near = pick.at[pl.ds(0, faces)]
-    pick_far = pick.at[pl.ds(faces, slots)]
-
     field0 = w_ref[...].astype(BF)
     traces0 = traces_of(field0)
-    put_forward(0, mm(traces0, send_hot[...]))
+    put_forward(0, pick_columns(traces0, send_hot, send_high, 0))
     jump0 = jump_grad_of(ct_ref[...])
-    jump0_s[...] = jump0
-    jump0_rows = to_rows(jump0).astype(BF)
-    put_backward(0, mm(pick_far[...], jump0_rows))
+    jump0_b = jump0.astype(BF)
+    put_backward(0, add_columns(jump0_b, link_hot_t, link_high, 6, far_count))
     pl.semaphore_wait(barrier, expected)
     start_exchange(0)
 
-    for base in range(0, faces, 256):
-        pick[pl.ds(base, 256), :] = one_hot_rows(partner, base, 256)
-    near[...] = mm(traces0, pick_near[...]) - traces0.astype(F32)
-    grad_near[...] = mm(pick_near[...], jump0_rows)
+    near[...] = pick_columns(traces0, link_hot, link_high, 0) - to_wide(
+        traces0.astype(F32), elements
+    )
+    grad_near[...] = add_columns(jump0_b, link_hot_t, link_high, 0, 6) - to_tall(
+        jump0, elements
+    )
 
     e1 = hot((iota((1024, 64), 0) & 63) == iota((1024, 64), 1))
     e1t = hot((iota((64, 1024), 1) & 63) == iota((64, 1024), 0))
@@ -356,18 +381,19 @@
     base0 = w_ref[...] + time_step * (volume0 + ungroup(clo, 0))
 
     wait_exchange(0)
-    jump = near[...] + mm(got_forward(0), pick_far[...])
+    jump = near[...] + pick_columns(got_forward(0), link_hot, link_high, 6)
     flux = mix(flux_ref, lift_gain * jump, False)
-    middle = base0 + time_step * lift(face_t, flux, elements)
+    middle = base0 + time_step * lift(face_t, to_tall(flux, elements))
     middle_s[...] = middle
-    rows = grad_near[...] + mm(send_hot[...], got_backward(0))
-    trace_grad = jnp.transpose(rows)[:80] - jump0_s[...]
-    adj_lift = lift(face_t, trace_grad, elements)
+    trace_grad = grad_near[...] + add_columns(
+        got_backward(0), send_hot_t, send_high, 0, 6
+    )
+    adj_lift = lift(face_t, trace_grad)
 
     field1 = middle.astype(BF)
     traces1 = traces_of(field1)
     traces_s[...] = traces1
-    put_forward(1, mm(traces1, send_hot[...]))
+    put_forward(1, pick_columns(traces1, send_hot, send_high, 0))
     volume1 = mm(vol_op_ref[...], field1)
     x_in[...] = group_rows([field1.astype(F32), volume1], 256)
     g_in[...] = group_rows([ct_ref[...]], 128)
@@ -390,16 +416,19 @@
     adj_mid = 0.5 * ct + 0.5 * time_step * (input_part(ct) + adj_lift)
     adj_mid_s[...] = adj_mid
     jump1 = jump_grad_of(adj_mid)
-    jump1_s[...] = jump1
-    jump1_rows = to_rows(jump1).astype(BF)
-    put_backward(1, mm(pick_far[...], jump1_rows))
+    jump1_b = jump1.astype(BF)
+    put_backward(1, add_columns(jump1_b, link_hot_t, link_high, 6, far_count))
     start_exchange(1)
 
     final_ref[...] = 0.5 * w_ref[...] + 0.5 * (
         middle_s[...] + time_step * (volume1 + ungroup(clo, 0))
     )
-    near[...] = mm(traces_s[...], pick_near[...]) - traces_s[...].astype(F32)
-    grad_near[...] = mm(pick_near[...], jump1_rows)
+    near[...] = pick_columns(traces_s[...], link_hot, link_high, 0) - to_wide(
+        traces_s[...].astype(F32), elements
+    )
+    grad_near[...] = add_columns(jump1_b, link_hot_t, link_high, 0, 6) - to_tall(
+        jump1, elements
+    )
     g_in[...] = group_rows([adj_mid], 128)
     x_grad[...] = jnp.zeros_like(x_grad)
 
@@ -412,12 +441,13 @@
     adj_ref[...] = 0.5 * ct_ref[...] + adj_mid + time_step * input_part(adj_mid)
 
     wait_exchange(1)
-    jump = near[...] + mm(got_forward(1), pick_far[...])
+    jump = near[...] + pick_columns(got_forward(1), link_hot, link_high, 6)
     flux = mix(flux_ref, lift_gain * jump, False)
-    final_ref[...] += 0.5 * time_step * lift(face_t, flux, elements)
-    rows = grad_near[...] + mm(send_hot[...], got_backward(1))
-    trace_grad = jnp.transpose(rows)[:80] - jump1_s[...]
-    adj_ref[...] += time_step * lift(face_t, trace_grad, elements)
+    final_ref[...] += 0.5 * time_step * lift(face_t, to_tall(flux, elements))
+    trace_grad = grad_near[...] + add_columns(
+        got_backward(1), send_hot_t, send_high, 0, 6
+    )
+    adj_ref[...] += time_step * lift(face_t, trace_grad)
 
 
 def body(
@@ -449,8 +479,10 @@
         in_specs=[vmem] * 8 + [smem, vmem, smem] + [vmem] * 2,
         out_specs=(vmem, vmem),
         scratch_shapes=[
-            pltpu.VMEM((faces + slots, faces), BF),
-            pltpu.VMEM((faces, slots), BF),
+            pltpu.VMEM((256, faces), BF),
+            pltpu.VMEM((faces, 256), BF),
+            pltpu.VMEM((256, slots), BF),
+            pltpu.VMEM((slots, 256), BF),
             pltpu.VMEM((1024, 256), BF),
             pltpu.VMEM((256, 1024), BF),
             pltpu.VMEM((256, 256), BF),
@@ -463,11 +495,9 @@
             pltpu.VMEM((4 * elements, 256), F32),
             pltpu.VMEM((4, 4 * elements, 256), BF),
             pltpu.VMEM((4, 4 * elements, 256), BF),
-            pltpu.VMEM((80, faces), BF),
+            pltpu.VMEM((480, elements), BF),
             pltpu.VMEM((80, faces), F32),
-            pltpu.VMEM((faces, 128), F32),
-            pltpu.VMEM((80, faces), F32),
-            pltpu.VMEM((80, faces), F32),
+            pltpu.VMEM((480, elements), F32),
             pltpu.VMEM(initial_state.shape, F32),
             pltpu.VMEM(initial_state.shape, F32),
             pltpu.VMEM((2, slots, 256), BF),

time: 35 us -> 29.8 us (0.85)
  Pallas kernels: 31.7 us -> 26.5 us
    pallas_call x1, Pallas kernels: 31.7 us -> 26.5 us  [body(): pl.pallas_call(functools.partial(kernel, n_dom, n_sub), out_shape=(state,...]
where the time goes in v3:
time: 29.8 us; the launch traced here: 29.6 us
  Pallas kernels  26.5 us (89%)
  local copies, waits for them, and re-layouts  2.49 us (8%)
  between operations  0.65 us (2%)
    pallas_call x1, Pallas kernels, body(): pl.pallas_call(functools.partial(kernel, n_dom, n_sub), out_shape=(state,...  26.5 us
    unnamed x4, local copies, waits for them, and re-layouts  2.49 us

profile of v3, /device:TPU:0, one launch (start us, length us, event | category | flops | bytes accessed | tf_op | source)
XLA Modules:
  0.0 29.6 jit_solution(17496985530906250785)
XLA Ops:
  0.6 26.5 %shard_map.140 = (f32[320,256]{1,0:T(8,128)}, f32[320,256]{1,0:T(8,128)}) custom-call(f32[320,256]{1,0:T(8,128)} %w_ref.1, f32[320,256]{1,0:T(8,128)} %ct_ref.1, bf16[320,320]{1,0:T(8,128)(2,1)} %vol_op_ref.1, bf16[10,64]{1,0:T(8,128)(2,1)} %bitcast.3, f32[1,64]{1,0:T(1,128)} %bitcast.4, bf16[64,64]{1,0:T(8,128)(2,1)} %mid_w_ref.1, f32[1,64]{1,0:T(1,128)} %bitcast.5, ...), custom_call_target="tpu_custom_call" | custom-call | flops 8000000000 | bytes 4000000 | tf_op jit(solution)/shard_map/pallas_call | solution.py:476
  27.1 0.0 copy-start
  27.1 1.8 %copy.17 = f32[320,256]{1,0:T(8,128)} copy(f32[320,256]{1,0:T(8,128)} %get-tuple-element.4) | data formatting | bytes 655360
  28.9 0.0 copy-done
  28.9 0.7 %copy.18 = f32[320,256]{1,0:T(8,128)} copy(f32[320,256]{1,0:T(8,128)S(1)} %copy-done) | data formatting | bytes 655360
Async XLA Ops:
  27.1 1.8 %copy-start = (f32[320,256]{1,0:T(8,128)S(1)}, f32[320,256]{1,0:T(8,128)}, u32[]{:S(2)}) copy-start(f32[320,256]{1,0:T(8,128)} %get-tuple-element.5) | copy-start | bytes 983044

commit v4 on v3

--- a/solution.py
+++ b/solution.py
@@ -377,7 +377,7 @@
         clo[...] += mm(h2.astype(BF), o16t[columns_of(sub), :])
         return carry
 
-    lax.fori_loop(0, 4, forward_step, 0)
+    lax.fori_loop(0, 4, forward_step, 0, unroll=True)
     base0 = w_ref[...] + time_step * (volume0 + ungroup(clo, 0))
 
     wait_exchange(0)
@@ -406,7 +406,7 @@
         back(sub, 1.0 - h1 * h1, 1.0 - h2 * h2)
         return carry
 
-    lax.fori_loop(0, 4, both_step, 0)
+    lax.fori_loop(0, 4, both_step, 0, unroll=True)
 
     def input_part(adjoint):
         field_grad, volume_grad = ungroup(x_grad, 0), ungroup(x_grad, 1)
@@ -436,7 +436,7 @@
         back(sub, slope1[sub].astype(F32), slope2[sub].astype(F32))
         return carry
 
-    lax.fori_loop(0, 4, back_step, 0)
+    lax.fori_loop(0, 4, back_step, 0, unroll=True)
     adj_mid = adj_mid_s[...]
     adj_ref[...] = 0.5 * ct_ref[...] + adj_mid + time_step * input_part(adj_mid)
 
@@ -448,6 +448,23 @@
         got_backward(1), send_hot_t, send_high, 0, 6
     )
     adj_ref[...] += time_step * lift(face_t, trace_grad)
+
+
+def hand_over(final_ref, adj_ref, final_out, adj_out, sems):
+    half = final_ref.shape[0] // 2
+    copies = []
+    for i, (source, target) in enumerate(((final_ref, final_out), (adj_ref, adj_out))):
+        for part in range(2):
+            rows = pl.ds(part * half, half)
+            copies.append(
+                pltpu.make_async_copy(
+                    source.at[rows], target.at[rows], sems.at[2 * i + part]
+                )
+            )
+    for copy in copies:
+        copy.start()
+    for copy in copies:
+        copy.wait()
 
 
 def body(
@@ -473,7 +490,7 @@
     vmem = pl.BlockSpec(memory_space=pltpu.VMEM)
     smem = pl.BlockSpec(memory_space=pltpu.SMEM)
     state = jax.ShapeDtypeStruct(initial_state.shape, F32)
-    return pl.pallas_call(
+    results = pl.pallas_call(
         functools.partial(kernel, n_dom, n_sub),
         out_shape=(state, state),
         in_specs=[vmem] * 8 + [smem, vmem, smem] + [vmem] * 2,
@@ -529,6 +546,15 @@
         partner,
     )
 
+    return pl.pallas_call(
+        hand_over,
+        out_shape=(state, state),
+        in_specs=[pl.BlockSpec(memory_space=pl.ANY)] * 2,
+        out_specs=(pl.BlockSpec(memory_space=pl.ANY),) * 2,
+        scratch_shapes=[pltpu.SemaphoreType.DMA((4,))],
+        compiler_params=pltpu.CompilerParams(vmem_limit_bytes=56 * 1024 * 1024),
+    )(*results)
+
 
 def solution(mesh):
     return jax.shard_map(

time: 29.8 us -> 45.9 us (1.54)
  Pallas kernels: 26.5 us -> 44.9 us
  local copies, waits for them, and re-layouts: 2.49 us -> 0 us
    pallas_call x0 -> x1, Pallas kernels: none -> 21 us  [body(): pl.pallas_call(hand_over, out_shape=(state, state), in_specs=[pl.BlockSpe...]
    pallas_call x1, Pallas kernels: 26.5 us -> 23.9 us  [body(): pl.pallas_call(functools.partial(kernel, n_dom, n_sub), out_shape=(state,...]
    unnamed x4 -> x0, local copies, waits for them, and re-layouts: 2.49 us -> none
where the time goes in v4:
time: 45.9 us; the launch traced here: 45.7 us
  Pallas kernels  44.9 us (98%)
  between operations  0.8 us (2%)
    pallas_call x1, Pallas kernels, body(): pl.pallas_call(functools.partial(kernel, n_dom, n_sub), out_shape=(state,...  23.9 us
    pallas_call x1, Pallas kernels, body(): pl.pallas_call(hand_over, out_shape=(state, state), in_specs=[pl.BlockSpe...  21 us

profile of v4, /device:TPU:0, one launch (start us, length us, event | category | flops | bytes accessed | tf_op | source)
XLA Modules:
  0.0 45.7 jit_solution(5068553465037203305)
XLA Ops:
  0.6 23.9 %shard_map.140 = (f32[320,256]{1,0:T(8,128)}, f32[320,256]{1,0:T(8,128)}) custom-call(f32[320,256]{1,0:T(8,128)} %w_ref.1, f32[320,256]{1,0:T(8,128)} %ct_ref.1, bf16[320,320]{1,0:T(8,128)(2,1)} %vol_op_ref.1, bf16[10,64]{1,0:T(8,128)(2,1)} %bitcast.3, f32[1,64]{1,0:T(1,128)} %bitcast.4, bf16[64,64]{1,0:T(8,128)(2,1)} %mid_w_ref.1, f32[1,64]{1,0:T(1,128)} %bitcast.5, ...), custom_call_target="tpu_custom_call" | custom-call | flops 8000000000 | bytes 4000000 | tf_op jit(solution)/shard_map/pallas_call | solution.py:493
  24.6 21.0 %shard_map.141 = (f32[320,256]{1,0:T(8,128)}, f32[320,256]{1,0:T(8,128)}) custom-call(f32[320,256]{1,0:T(8,128)} %get-tuple-element.4.final_ref, f32[320,256]{1,0:T(8,128)} %get-tuple-element.5.adj_ref), custom_call_target="tpu_custom_call" | custom-call | tf_op jit(solution)/shard_map/pallas_call | solution.py:549

commit v5 on v3

--- a/solution.py
+++ b/solution.py
@@ -377,7 +377,7 @@
         clo[...] += mm(h2.astype(BF), o16t[columns_of(sub), :])
         return carry
 
-    lax.fori_loop(0, 4, forward_step, 0)
+    lax.fori_loop(0, 4, forward_step, 0, unroll=True)
     base0 = w_ref[...] + time_step * (volume0 + ungroup(clo, 0))
 
     wait_exchange(0)
@@ -406,7 +406,7 @@
         back(sub, 1.0 - h1 * h1, 1.0 - h2 * h2)
         return carry
 
-    lax.fori_loop(0, 4, both_step, 0)
+    lax.fori_loop(0, 4, both_step, 0, unroll=True)
 
     def input_part(adjoint):
         field_grad, volume_grad = ungroup(x_grad, 0), ungroup(x_grad, 1)
@@ -436,7 +436,7 @@
         back(sub, slope1[sub].astype(F32), slope2[sub].astype(F32))
         return carry
 
-    lax.fori_loop(0, 4, back_step, 0)
+    lax.fori_loop(0, 4, back_step, 0, unroll=True)
     adj_mid = adj_mid_s[...]
     adj_ref[...] = 0.5 * ct_ref[...] + adj_mid + time_step * input_part(adj_mid)
 

time: 29.8 us -> 27.2 us (0.913)
  Pallas kernels: 26.5 us -> 23.9 us
    pallas_call x1, Pallas kernels: 26.5 us -> 23.9 us  [body(): pl.pallas_call(functools.partial(kernel, n_dom, n_sub), out_shape=(state,...]
where the time goes in v5:
time: 27.2 us; the launch traced here: 27.1 us
  Pallas kernels  23.9 us (88%)
  local copies, waits for them, and re-layouts  2.49 us (9%)
  between operations  0.65 us (2%)
    pallas_call x1, Pallas kernels, body(): pl.pallas_call(functools.partial(kernel, n_dom, n_sub), out_shape=(state,...  23.9 us
    unnamed x4, local copies, waits for them, and re-layouts  2.49 us

profile of v5, /device:TPU:0, one launch (start us, length us, event | category | flops | bytes accessed | tf_op | source)
XLA Modules:
  0.0 27.1 jit_solution(504144548460713092)
XLA Ops:
  0.6 23.9 %shard_map.140 = (f32[320,256]{1,0:T(8,128)}, f32[320,256]{1,0:T(8,128)}) custom-call(f32[320,256]{1,0:T(8,128)} %w_ref.1, f32[320,256]{1,0:T(8,128)} %ct_ref.1, bf16[320,320]{1,0:T(8,128)(2,1)} %vol_op_ref.1, bf16[10,64]{1,0:T(8,128)(2,1)} %bitcast.3, f32[1,64]{1,0:T(1,128)} %bitcast.4, bf16[64,64]{1,0:T(8,128)(2,1)} %mid_w_ref.1, f32[1,64]{1,0:T(1,128)} %bitcast.5, ...), custom_call_target="tpu_custom_call" | custom-call | flops 8000000000 | bytes 4000000 | tf_op jit(solution)/shard_map/pallas_call | solution.py:476
  24.6 0.0 copy-start
  24.6 1.8 %copy.17 = f32[320,256]{1,0:T(8,128)} copy(f32[320,256]{1,0:T(8,128)} %get-tuple-element.4) | data formatting | bytes 655360
  26.4 0.0 copy-done
  26.4 0.7 %copy.18 = f32[320,256]{1,0:T(8,128)} copy(f32[320,256]{1,0:T(8,128)S(1)} %copy-done) | data formatting | bytes 655360
Async XLA Ops:
  24.6 1.8 %copy-start = (f32[320,256]{1,0:T(8,128)S(1)}, f32[320,256]{1,0:T(8,128)}, u32[]{:S(2)}) copy-start(f32[320,256]{1,0:T(8,128)} %get-tuple-element.5) | copy-start | bytes 983044
